TPU v7x, 32 devices: a whole 2x2x4 slice. The times are simulated.
32 devices in a mesh: leaf: 4 (over y, x), row: 2 (over core), col: 4 (over z).
Axes of the slice: x: 2, y: 2, z: 4, core: 2. Of those that a mesh axis runs over, the one named last changes fastest.
Arguments:
- sec_rhs: float32 [4, 7, 64, 2048], P('leaf', None, None, 'row'), may hold values from -6 to 6
- sec_inv: float32 [4, 7, 2048, 2048], P('leaf', None, 'row', 'col'), as said below
- sec_low: float32 [4, 10, 2048, 2048], P('leaf', None, 'row', 'col'), may hold values from -0.09375 to 0.09375
- sec_top: float32 [4, 7, 2048, 2048], P('leaf', None, 'row', 'col'), may hold values from -0.046875 to 0.046875
- sec_rows: int32 [4, 7, 16], P('leaf'), may hold values from 0 to 47, as said below
- top_rhs: float32 [7, 64, 2048], P(None, None, 'row'), may hold values from -6 to 6
- top_inv: float32 [7, 2048, 2048], P(None, 'row', 'col'), as said below
- top_low: float32 [10, 2048, 2048], P(None, 'row', 'col'), may hold values from -0.09375 to 0.09375
- sec_parent: int32 [4], replicated, may hold values from 0 to 3, as said below
- top_parent: int32 [4], replicated, may hold values from 0 to 1, as said below
Outputs:
- sec_sol: float32 [4, 7, 64, 2048], P('leaf', None, None, 'row')
- top_sol: float32 [7, 64, 2048], P(None, None, 'row')
Inputs may be any that keep to these rules, and one draw needn't show every extreme that they name: `sec_rows`: within each list the 16 values are distinct. `sec_parent`: each of 0, 1, 2, 3 appears exactly once. `top_parent`: each of 0 and 1 appears exactly twice. `sec_inv`: dense matrices with a positive diagonal; nothing more is promised of their entries. `top_inv`: dense matrices with a positive diagonal; nothing more is promised of their entries.
All inputs are finite; a program needn't handle non-finite values.
Results may differ from a plain program's by a relative error of at most 0.00012.
Values sent between devices are 32-bit elements; how exact they have to be, the bound alone decides.
A program may use at most 192 MiB of HBM per device.

v0:
```python
import jax
import jax.numpy as jnp
from jax import lax
from jax.sharding import PartitionSpec as P

BLOCK = 128


def apply_block(vectors, matrices):
    return jnp.einsum("btc,brc->btr", vectors, matrices, precision=lax.Precision.HIGHEST)


def per_device(
    sec_rhs, sec_inv, sec_low, sec_top, sec_rows, top_rhs, top_inv, top_low, sec_parent, top_parent
):
    parts_row = lax.axis_size("row")
    here_row = lax.axis_index("row")
    here_col = lax.axis_index("col")
    here_leaf = lax.axis_index("leaf")
    rows_here = sec_rhs.shape[-1]
    cols_here = sec_inv.shape[-1]
    width = rows_here * parts_row
    blocks = width // BLOCK
    nrhs = sec_rhs.shape[2]

    def own_cols(full):
        return lax.dynamic_slice_in_dim(full, here_col * cols_here, cols_here, 2)

    def solve_level(known, partial_value, inverse):
        if partial_value is None:
            y_rows = known
        else:
            y_rows = known - lax.psum(partial_value, "col")
        y_full = lax.all_gather(y_rows, "row", axis=2, tiled=True)
        x_part = apply_block(own_cols(y_full), inverse)
        x_rows = lax.psum(x_part, "col")
        x_full = lax.all_gather(x_rows, "row", axis=2, tiled=True)
        return (x_rows, x_full)

    right_side = sec_rhs[0]
    inverse = sec_inv[0]
    lower = sec_low[0]
    rows_leaf, full_leaf = solve_level(right_side[0:4], None, inverse[0:4])
    cols_leaf = own_cols(full_leaf)
    upward = apply_block(cols_leaf, lower[0:4])
    acc_mid = upward.reshape(2, 2, nrhs, rows_here).sum(1)
    acc_root = apply_block(cols_leaf, lower[4:8]).sum(0, keepdims=True)
    rows_mid, full_mid = solve_level(right_side[4:6], acc_mid, inverse[4:6])
    cols_mid = own_cols(full_mid)
    acc_root = acc_root + apply_block(cols_mid, lower[8:10]).sum(0, keepdims=True)
    rows_root, full_root = solve_level(right_side[6:7], acc_root, inverse[6:7])
    sec_out = jnp.concatenate([rows_leaf, rows_mid, rows_root], axis=0)[None]
    all_cols = jnp.concatenate([cols_leaf, cols_mid, own_cols(full_root)], axis=0)
    block_rows = sec_top.shape[2] // BLOCK
    contrib = apply_block(all_cols, sec_top[0]).reshape(7, nrhs, block_rows, BLOCK)
    mine = lax.dynamic_slice_in_dim(sec_rows[0], here_row * block_rows, block_rows, 1)
    section_ids = jnp.arange(sec_parent.shape[0], dtype=jnp.int32)
    parent_node = jnp.sum(jnp.where(section_ids == here_leaf, sec_parent, 0))
    grand_node = jnp.sum(jnp.where(jnp.arange(4, dtype=jnp.int32) == parent_node, top_parent, 0))
    path_which = mine // blocks
    node_of = jnp.where(path_which == 0, parent_node, jnp.where(path_which == 1, grand_node + 4, 6))
    sub_block = mine % blocks
    node_ids = jnp.arange(7, dtype=jnp.int32)
    block_ids = jnp.arange(blocks, dtype=jnp.int32)
    one_hot = (
        (node_of[:, :, None, None] == node_ids[None, None, :, None])
        & (sub_block[:, :, None, None] == block_ids[None, None, None, :])
    ).astype(jnp.float32)
    one_hot = one_hot.reshape(7, block_rows, 7, parts_row, blocks // parts_row)
    spread = jnp.einsum("jtkl,jknpm->pntml", contrib, one_hot, precision=lax.Precision.HIGHEST)
    spread = spread.reshape(parts_row, 7, nrhs, rows_here)
    total_update = lax.psum(spread, ("leaf", "row", "col"))
    top_update = lax.dynamic_index_in_dim(total_update, here_row, 0, keepdims=False)
    known_top = top_rhs - top_update
    earlier = jnp.sum(((sec_parent == parent_node) & (section_ids < here_leaf)).astype(jnp.int32))
    owner = (earlier == 0).astype(jnp.float32)
    known_own = lax.dynamic_slice_in_dim(known_top, parent_node, 1, 0)
    inverse_own = lax.dynamic_slice_in_dim(top_inv, parent_node, 1, 0)
    rows_own, full_own = solve_level(known_own, None, inverse_own)
    lower_pair = lax.dynamic_slice_in_dim(top_low, 2 * parent_node, 2, 0)
    reaches = jnp.einsum(
        "tc,brc->btr", own_cols(full_own)[0], lower_pair, precision=lax.Precision.HIGHEST
    )
    mid_hot = (jnp.arange(2, dtype=jnp.int32) == grand_node).astype(jnp.float32)
    slot_hot = (jnp.arange(4, dtype=jnp.int32) == parent_node).astype(jnp.float32)
    sol_term = slot_hot[:, None, None] * rows_own * owner
    mid_term = mid_hot[:, None, None] * reaches[0:1] * owner
    root_term = reaches[1:2] * owner
    rows_three, acc_four, acc_top = lax.psum((sol_term, mid_term, root_term), "leaf")
    rows_four, full_four = solve_level(known_top[4:6], acc_four, top_inv[4:6])
    acc_top = acc_top + apply_block(own_cols(full_four), top_low[8:10]).sum(0, keepdims=True)
    rows_five, full_five = solve_level(known_top[6:7], acc_top, top_inv[6:7])
    top_out = jnp.concatenate([rows_three, rows_four, rows_five], axis=0)
    return (sec_out, top_out)


def solution(mesh):
    placed = (
        P("leaf", None, None, "row"),
        P("leaf", None, "row", "col"),
        P("leaf", None, "row", "col"),
        P("leaf", None, "row", "col"),
        P("leaf", None, None),
        P(None, None, "row"),
        P(None, "row", "col"),
        P(None, "row", "col"),
        P(),
        P(),
    )
    return jax.shard_map(
        per_device,
        mesh=mesh,
        in_specs=placed,
        out_specs=(P("leaf", None, None, "row"), P(None, None, "row")),
        check_vma=False,
    )
```

profile of v0, /device:TPU:24, one launch (start us, length us, event | category | flops | bytes accessed | tf_op | source)
XLA Modules:
  0.0 803.6 jit_solution(7235727940274795039)
XLA Ops:
  7.2 2.3 slice.73
  9.6 12.4 %all-gather.18.cloned.1.call-done = f32[1,4,64,2048]{3,2,1,0:T(8,128)} async-done(((f32[1,4,64,1024]{3,2,1,0:T(8,128)}), f32[1,4,64,2048]{3,2,1,0:T(8,128)}) %all-gather.18.cloned.1.call-update) | async-done | bytes 2097168 | tf_op jit(solution)/shard_map/all_gather | solution.py:34
  22.0 12.5 %fusion.6 = f32[4,64,1024]{2,1,0:T(8,128)} fusion(f32[1,7,1024,512]{3,2,1,0:T(8,128)} %param.11, f32[1,4,64,2048]{3,2,1,0:T(8,128)} %all-gather.18.cloned.1.call-done, s32[]{:T(128)S(6)} %select_n.70), kind=kOutput, calls=%fused_computation.6 | convolution fusion | flops 1610612736 | bytes 9961476 | tf_op jit(solution)/shard_map/btc,brc->btr/dot_general | solution.py:10
  34.6 51.3 %all-reduce.14.cloned.1.call-done = f32[4,64,1024]{2,1,0:T(8,128)} async-done(((f32[4,64,1024]{2,1,0:T(8,128)}), f32[4,64,1024]{2,1,0:T(8,128)}) %all-reduce.14.cloned.1.call-update) | async-done | bytes 1048592 | tf_op jit(solution)/shard_map/psum | solution.py:36
  85.9 13.3 %all-gather.8.cloned.1.call-done = f32[4,64,2048]{2,1,0:T(8,128)} async-done(((f32[4,64,1024]{2,1,0:T(8,128)}), f32[4,64,2048]{2,1,0:T(8,128)}) %all-gather.8.cloned.1.call-update) | async-done | bytes 2097168 | tf_op jit(solution)/shard_map/all_gather | solution.py:37
  99.3 1.1 constant_dynamic-slice_fusion.4
  100.3 11.3 %bitcast_reduce_fusion = f32[2,64,1024]{2,1,0:T(8,128)} fusion(f32[4,64,512]{2,1,0:T(8,128)S(1)} %constant_dynamic-slice_fusion.4, f32[1,10,1024,512]{3,2,1,0:T(8,128)} %param.12), kind=kOutput, calls=%fused_computation.47 | convolution fusion | flops 1610743808 | bytes 9437184 | tf_op jit(solution)/shard_map/btc,brc->btr/dot_general | solution.py:10
  111.7 38.3 %all-reduce.16.cloned.1.call-done = f32[2,64,1024]{2,1,0:T(8,128)} async-done(((f32[2,64,1024]{2,1,0:T(8,128)}), f32[2,64,1024]{2,1,0:T(8,128)}) %all-reduce.16.cloned.1.call-update) | async-done | bytes 524304 | tf_op jit(solution)/shard_map/psum | solution.py:33
  150.1 2.1 bitcast_subtract_fusion.1
  152.4 10.2 %all-gather.10.cloned.1.call-done = f32[2,64,2048]{2,1,0:T(8,128)} async-done(((f32[2,64,1024]{2,1,0:T(8,128)}), f32[2,64,2048]{2,1,0:T(8,128)}) %all-gather.10.cloned.1.call-update) | async-done | bytes 1048592 | tf_op jit(solution)/shard_map/all_gather | solution.py:34
  162.6 7.1 fusion.13
  169.8 38.4 %all-reduce.18.cloned.1.call-done = f32[2,64,1024]{2,1,0:T(8,128)} async-done(((f32[2,64,1024]{2,1,0:T(8,128)}), f32[2,64,1024]{2,1,0:T(8,128)}) %all-reduce.18.cloned.1.call-update) | async-done | bytes 524304 | tf_op jit(solution)/shard_map/psum | solution.py:36
  208.8 1.3 fusion.97
  210.9 10.5 %fusion.44 = f32[64,1024]{1,0:T(8,128)S(1)} fusion(f32[4,64,512]{2,1,0:T(8,128)S(1)} %constant_dynamic-slice_fusion.4, f32[1,10,1024,512]{3,2,1,0:T(8,128)} %param.12), kind=kOutput, calls=%fused_computation.41 | convolution fusion | flops 1610612736 | bytes 9175040 | tf_op jit(solution)/shard_map/btc,brc->btr/dot_general | solution.py:10
  222.4 7.0 fusion.59
  230.1 34.6 %all-reduce.20.cloned.1.call-done = f32[1,64,1024]{2,1,0:T(8,128)} async-done(((f32[1,64,1024]{2,1,0:T(8,128)}), f32[1,64,1024]{2,1,0:T(8,128)}) %all-reduce.20.cloned.1.call-update) | async-done | bytes 262160 | tf_op jit(solution)/shard_map/psum | solution.py:33
  264.7 1.1 bitcast_subtract_fusion.2
  265.8 2.2 all_gather.37
  267.9 4.4 fusion.47
  272.5 35.0 %all-reduce.22.cloned.1.call-done = f32[1,64,1024]{2,1,0:T(8,128)} async-done(((f32[1,64,1024]{2,1,0:T(8,128)}), f32[1,64,1024]{2,1,0:T(8,128)}) %all-reduce.22.cloned.1.call-update) | async-done | bytes 262160 | tf_op jit(solution)/shard_map/psum | solution.py:36
  307.5 2.6 all_gather.38
  310.2 17.5 %fusion = f32[7,64,1024]{2,1,0:T(8,128)S(1)} fusion(f32[1,7,1024,512]{3,2,1,0:T(8,128)} %param.13, f32[1,64,512]{2,1,0:T(8,128)S(1)} %constant_dynamic-slice_fusion.1, f32[2,64,512]{2,1,0:T(8,128)S(1)} %constant_dynamic-slice_fusion.3, f32[4,64,512]{2,1,0:T(8,128)S(1)} %constant_dynamic-slice_fusion.4), kind=kOutput, calls=%fused_computation | convolution fusion | flops 2819031040 | bytes 17432576 | tf_op jit(solution)/shard_map/btc,brc->btr/dot_general | solution.py:10
  328.0 4.9 convolution_bitcast_fusion
  333.0 4.7 reshape.130
  339.7 136.8 %all-reduce.24.cloned.1.call-done = f32[2,7,64,1024]{3,2,0,1:T(8,128)} async-done(((f32[2,7,64,1024]{3,2,0,1:T(8,128)}), f32[2,7,64,1024]{3,2,0,1:T(8,128)}) %all-reduce.24.cloned.1.call-update) | async-done | bytes 3670032 | tf_op jit(solution)/shard_map/psum | solution.py:72
  476.5 2.4 bitcast_subtract_fusion
  479.0 2.2 all_gather.39
  481.1 4.4 fusion.50
  485.6 1.3 fusion.99
  489.4 31.2 %all-reduce.26.cloned.1.call-done = f32[1,64,1024]{2,1,0:T(8,128)} async-done(((f32[1,64,1024]{2,1,0:T(8,128)}), f32[1,64,1024]{2,1,0:T(8,128)}) %all-reduce.26.cloned.1.call-update) | async-done | bytes 262160 | tf_op jit(solution)/shard_map/psum | solution.py:36
  520.6 2.8 all_gather.40
  523.3 6.3 fusion.32
  531.4 1.2 multiply_multiply_fusion
  532.6 66.6 %all-reduce.36.cloned.1.call-done = (f32[1,64,1024]{2,1,0:T(8,128)}, f32[2,64,1024]{2,1,0:T(8,128)}, f32[4,64,1024]{2,1,0:T(8,128)}) async-done(((f32[1,64,1024]{2,1,0:T(8,128)}, f32[2,64,1024]{2,1,0:T(8,128)}, f32[4,64,1024]{2,1,0:T(8,128)}), (f32[1,64,1024]{2,1,0:T(8,128)}, f32[2,64,1024]{2,1,0:T(8,128)}, f32[4,64,1024]{2,1,0:T(8,128)})) %all-reduce.36.cloned.1.call-update) | async-done | bytes 1835024 | tf_op jit(solution)/shard_map/psum | solution.py:89
  599.3 39.6 %all-reduce.28.cloned.1.call-done = f32[2,64,1024]{2,1,0:T(8,128)} async-done(((f32[2,64,1024]{2,1,0:T(8,128)}), f32[2,64,1024]{2,1,0:T(8,128)}) %all-reduce.28.cloned.1.call-update) | async-done | bytes 524304 | tf_op jit(solution)/shard_map/psum | solution.py:33
  638.9 1.9 slice_subtract_fusion
  640.9 10.3 %all-gather.14.cloned.1.call-done = f32[2,64,2048]{2,1,0:T(8,128)} async-done(((f32[2,64,1024]{2,1,0:T(8,128)}), f32[2,64,2048]{2,1,0:T(8,128)}) %all-gather.14.cloned.1.call-update) | async-done | bytes 1048592 | tf_op jit(solution)/shard_map/all_gather | solution.py:34
  651.3 7.1 fusion.17
  658.5 38.3 %all-reduce.30.cloned.1.call-done = f32[2,64,1024]{2,1,0:T(8,128)} async-done(((f32[2,64,1024]{2,1,0:T(8,128)}), f32[2,64,1024]{2,1,0:T(8,128)}) %all-reduce.30.cloned.1.call-update) | async-done | bytes 524304 | tf_op jit(solution)/shard_map/psum | solution.py:36
  696.9 11.6 %all-gather.16.cloned.1.call-done = f32[2,64,2048]{2,1,0:T(8,128)} async-done(((f32[2,64,1024]{2,1,0:T(8,128)}), f32[2,64,2048]{2,1,0:T(8,128)}) %all-gather.16.cloned.1.call-update) | async-done | bytes 1048592 | tf_op jit(solution)/shard_map/all_gather | solution.py:37
  708.5 7.2 fusion.38
  715.7 35.2 %all-reduce.32.cloned.1.call-done = f32[1,64,1024]{2,1,0:T(8,128)} async-done(((f32[1,64,1024]{2,1,0:T(8,128)}), f32[1,64,1024]{2,1,0:T(8,128)}) %all-reduce.32.cloned.1.call-update) | async-done | bytes 262160 | tf_op jit(solution)/shard_map/psum | solution.py:33
  751.0 1.0 slice_subtract_fusion.1
  752.0 2.3 all_gather.43
  754.3 4.4 fusion.53
  758.8 2.3 maximum_bitcast_fusion
  761.1 32.9 %all-reduce.34.cloned.1.call-done = f32[1,64,1024]{2,1,0:T(8,128)} async-done(((f32[1,64,1024]{2,1,0:T(8,128)}), f32[1,64,1024]{2,1,0:T(8,128)}) %all-reduce.34.cloned.1.call-update) | async-done | bytes 262160 | tf_op jit(solution)/shard_map/psum | solution.py:36
  794.0 2.3 pad_maximum_fusion
  (69 shorter events, 7.1 us)
Async XLA Ops:
  7.2 203.6 %copy-start = (s32[1,7,16]{2,0,1:T(1,128)S(1)}, s32[1,7,16]{2,0,1:T(1,128)}, u32[]{:S(2)}) copy-start(s32[1,7,16]{2,0,1:T(1,128)} %param.14) | copy-start | bytes 1348
  7.2 14.8 %all-gather.18.cloned.1.call-start = ((), (), s32[]{:S(2)}) async-start(), calls=%async_computation.16 | async-start | bytes 3145728 | tf_op jit(solution)/shard_map/all_gather | solution.py:34
  9.6 76.3 %all-reduce.14.cloned.1.call-start = ((), (), s32[]{:S(2)}) async-start(), calls=%async_computation | async-start | bytes 2097152 | tf_op jit(solution)/shard_map/psum | solution.py:36
  34.5 64.7 %all-gather.8.cloned.1.call-start = ((), (), s32[]{:S(2)}) async-start(), calls=%async_computation.1 | async-start | bytes 3145728 | tf_op jit(solution)/shard_map/all_gather | solution.py:37
  85.9 64.2 %all-reduce.16.cloned.1.call-start = ((), (), s32[]{:S(2)}) async-start(), calls=%async_computation.2 | async-start | bytes 1048576 | tf_op jit(solution)/shard_map/psum | solution.py:33
  111.7 96.5 %copy-start.7 = (s32[4]{0:T(128)S(1)}, s32[4]{0:T(128)}, u32[]{:S(2)}) copy-start(s32[4]{0:T(128)} %param.18) | copy-start | bytes 52
  111.7 97.2 %copy-start.8 = (s32[4]{0:T(128)S(1)}, s32[4]{0:T(128)}, u32[]{:S(2)}) copy-start(s32[4]{0:T(128)} %param.19) | copy-start | bytes 52
  111.7 50.9 %all-gather.10.cloned.1.call-start = ((), (), s32[]{:S(2)}) async-start(), calls=%async_computation.3 | async-start | bytes 1572864 | tf_op jit(solution)/shard_map/all_gather | solution.py:34
  152.2 56.0 %all-reduce.18.cloned.1.call-start = ((), (), s32[]{:S(2)}) async-start(), calls=%async_computation.4 | async-start | bytes 1048576 | tf_op jit(solution)/shard_map/psum | solution.py:36
  169.7 51.7 %all-gather.12.cloned.1.call-start = ((), (), s32[]{:S(2)}) async-start(), calls=%async_computation.5 | async-start | bytes 1572864 | tf_op jit(solution)/shard_map/all_gather | solution.py:37
  208.1 56.5 %all-reduce.20.cloned.1.call-start = ((), (), s32[]{:S(2)}) async-start(), calls=%async_computation.6 | async-start | bytes 524288 | tf_op jit(solution)/shard_map/psum | solution.py:33
  229.4 78.2 %all-reduce.22.cloned.1.call-start = ((), (), s32[]{:S(2)}) async-start(), calls=%async_computation.7 | async-start | bytes 524288 | tf_op jit(solution)/shard_map/psum | solution.py:36
  272.4 204.2 %all-reduce.24.cloned.1.call-start = ((), (), s32[]{:S(2)}) async-start(), calls=%async_computation.8 | async-start | bytes 7340032 | tf_op jit(solution)/shard_map/psum | solution.py:72
  337.7 182.9 %all-reduce.26.cloned.1.call-start = ((), (), s32[]{:S(2)}) async-start(), calls=%async_computation.9 | async-start | bytes 524288 | tf_op jit(solution)/shard_map/psum | solution.py:36
  485.6 113.6 %all-reduce.36.cloned.1.call-start = ((), (), s32[]{:S(2)}) async-start(), calls=%async_computation.17 | async-start | bytes 3670016 | tf_op jit(solution)/shard_map/psum | solution.py:89
  520.6 10.8 %copy-start.6 = (f32[1,64,1024]{2,1,0:T(8,128)S(1)}, f32[1,64,1024]{2,1,0:T(8,128)}, u32[]{:S(2)}) copy-start(f32[1,64,1024]{2,1,0:T(8,128)} %all-reduce.26.cloned.1.call-done) | copy-start | bytes 786436
  532.5 106.4 %all-reduce.28.cloned.1.call-start = ((), (), s32[]{:S(2)}) async-start(), calls=%async_computation.10 | async-start | bytes 1048576 | tf_op jit(solution)/shard_map/psum | solution.py:33
  599.3 52.0 %all-gather.14.cloned.1.call-start = ((), (), s32[]{:S(2)}) async-start(), calls=%async_computation.11 | async-start | bytes 1572864 | tf_op jit(solution)/shard_map/all_gather | solution.py:34
  640.9 55.9 %all-reduce.30.cloned.1.call-start = ((), (), s32[]{:S(2)}) async-start(), calls=%async_computation.12 | async-start | bytes 1048576 | tf_op jit(solution)/shard_map/psum | solution.py:36
  658.4 50.1 %all-gather.16.cloned.1.call-start = ((), (), s32[]{:S(2)}) async-start(), calls=%async_computation.13 | async-start | bytes 1572864 | tf_op jit(solution)/shard_map/all_gather | solution.py:37
  696.8 54.1 %all-reduce.32.cloned.1.call-start = ((), (), s32[]{:S(2)}) async-start(), calls=%async_computation.14 | async-start | bytes 524288 | tf_op jit(solution)/shard_map/psum | solution.py:33
  708.5 50.3 %copy-start.2 = (f32[4,64,1024]{2,1,0:T(8,128)S(1)}, f32[4,64,1024]{2,1,0:T(8,128)}, u32[]{:S(2)}) copy-start(f32[4,64,1024]{2,1,0:T(8,128)} %all-reduce.14.cloned.1.call-done) | copy-start | bytes 3145732
  708.5 50.3 %copy-start.3 = (f32[2,64,1024]{2,1,0:T(8,128)S(1)}, f32[2,64,1024]{2,1,0:T(8,128)}, u32[]{:S(2)}) copy-start(f32[2,64,1024]{2,1,0:T(8,128)} %all-reduce.18.cloned.1.call-done) | copy-start | bytes 1572868
  715.7 78.3 %all-reduce.34.cloned.1.call-start = ((), (), s32[]{:S(2)}) async-start(), calls=%async_computation.15 | async-start | bytes 524288 | tf_op jit(solution)/shard_map/psum | solution.py:36
  752.0 42.0 %copy-start.4 = (f32[2,64,1024]{2,1,0:T(8,128)S(1)}, f32[2,64,1024]{2,1,0:T(8,128)}, u32[]{:S(2)}) copy-start(f32[2,64,1024]{2,1,0:T(8,128)} %all-reduce.30.cloned.1.call-done) | copy-start | bytes 1572868
  752.0 42.0 %copy-start.5 = (f32[4,64,1024]{2,1,0:T(8,128)S(1)}, f32[4,64,1024]{2,1,0:T(8,128)}, u32[]{:S(2)}) copy-start(f32[4,64,1024]{2,1,0:T(8,128)} %get-tuple-element.4) | copy-start | bytes 3145732
  754.3 42.0 %copy-start.1 = (s32[1,7,16]{2,0,1:T(1,128)S(1)}, s32[1,7,16]{2,0,1:T(1,128)}, u32[]{:S(2)}) copy-start(s32[1,7,16]{2,0,1:T(1,128)} %param.14) | copy-start | bytes 1348
Sparse Core Ops, SparseCore 0:
  10.1 11.8 all-gather.17
  34.6 51.1 all-reduce.13
  87.5 11.7 all-gather.7
  111.8 38.2 all-reduce.15
  152.3 10.2 all-gather.9
  169.8 38.2 all-reduce.17
  209.7 10.2 all-gather.11
  229.5 35.1 all-reduce.19
  272.5 35.0 all-reduce.21
  337.8 138.6 all-reduce.23
  485.7 34.8 all-reduce.25
  532.7 66.5 all-reduce.35
  601.6 37.2 all-reduce.27
  641.0 10.2 all-gather.13
  658.5 38.2 all-reduce.29
  698.2 10.2 all-gather.15
  715.8 35.0 all-reduce.31
  758.9 35.0 all-reduce.33
where the time goes:
time: 814 us; the launch traced here: 804 us
  waiting for transfers between devices  636 us (78%)
  matrix products  105 us (13%)
  other arithmetic  21.2 us (3%)
  between operations  18.7 us (2%)
  blocking collectives  12 us (1%)
  local copies, waits for them, and re-layouts  9.65 us (1%)
    psum x6, waiting for transfers between devices, solve_level(): x_rows = lax.psum(x_part, 'col')  227 us
    psum x4, waiting for transfers between devices, solve_level(): y_rows = known - lax.psum(partial_value, 'col')  148 us
    psum x1, waiting for transfers between devices, per_device(): total_update = lax.psum(spread, ('leaf', 'row', 'col'))  137 us
    dot_general x11, matrix products, apply_block(): jnp.einsum('btc,brc->btr', vectors, matrices, precision=lax.Precision.HIG...  93.5 us
    psum x1, waiting for transfers between devices, per_device(): lax.psum((sol_term, mid_term, root_term), 'leaf')  66.6 us
    all_gather x3, waiting for transfers between devices, solve_level(): y_full = lax.all_gather(y_rows, 'row', axis=2, tiled=True)  32.9 us
    all_gather x3, waiting for transfers between devices, solve_level(): x_full = lax.all_gather(x_rows, 'row', axis=2, tiled=True)  25 us
  transfers between devices with their start and end apart: 18, of which 17 were waited for; matrix products, arithmetic and copies ran while one was open for 2% of the time, Pallas kernels for 0%

commit v1 on v0

v1 whole, which is shorter than its diff:
```python
import functools

import jax
import jax.numpy as jnp
from jax import lax
from jax.experimental import pallas as pl
from jax.experimental.pallas import tpu as pltpu
from jax.sharding import PartitionSpec as P

BLOCK = 128
MESH = pl.DeviceIdType.MESH


def apply_block(vectors, matrices):
    return jnp.einsum("btc,brc->btr", vectors, matrices, precision=lax.Precision.HIGH)


def place():
    return lax.axis_index("leaf"), lax.axis_index("row"), lax.axis_index("col")


def remote(src, dst, send, recv, target):
    return pltpu.make_async_remote_copy(
        src_ref=src, dst_ref=dst, send_sem=send, recv_sem=recv, device_id=target, device_id_type=MESH
    )


def reduce_kernel(cols, x_ref, o_ref, got, pair, send, recv, pair_send, pair_recv):
    leaf, row, col = place()
    per = cols // 2
    width = o_ref.shape[-1]
    holds = col // per == row
    barrier = pltpu.get_barrier_semaphore()

    @pl.when(holds)
    def _():
        for d in range(1, cols):
            pl.semaphore_signal(
                barrier, inc=1, device_id=(leaf, row, lax.rem(col + d, cols)), device_id_type=MESH
            )

    @pl.when(jnp.logical_not(holds))
    def _():
        pl.semaphore_signal(barrier, inc=1, device_id=(leaf, 1 - row, col), device_id_type=MESH)

    pl.semaphore_wait(barrier, per)

    def out_copy(j):
        return remote(
            x_ref.at[:, :, j * width : (j + 1) * width],
            got.at[col],
            send.at[j],
            recv.at[col],
            (leaf, row, row * per + j),
        )

    for j in range(per):
        @pl.when(row * per + j != col)
        def _():
            out_copy(j).start()

    across = remote(o_ref, pair, pair_send, pair_recv, (leaf, 1 - row, col))

    @pl.when(holds)
    def _():
        for j in range(per):
            @pl.when(row * per + j == col)
            def _():
                o_ref[...] = x_ref[:, :, j * width : (j + 1) * width]
        for d in range(1, cols):
            source = lax.rem(col + d, cols)
            remote(
                got.at[source], got.at[source], send.at[0], recv.at[source], (leaf, row, source)
            ).wait_recv()
            o_ref[...] += got[source]
        across.start()
        across.wait_send()

    @pl.when(jnp.logical_not(holds))
    def _():
        across.wait_recv()
        o_ref[...] = pair[...]

    for j in range(per):
        @pl.when(row * per + j != col)
        def _():
            out_copy(j).wait_send()


def gather_kernel(cols, x_ref, o_ref, got, send, recv):
    leaf, row, col = place()
    per = cols // 2
    width = x_ref.shape[-1]
    holds = col // per == row
    barrier = pltpu.get_barrier_semaphore()
    slot = lax.rem(col, per)
    for j in range(per):
        @pl.when(row * per + j != col)
        def _():
            pl.semaphore_signal(
                barrier, inc=1, device_id=(leaf, row, row * per + j), device_id_type=MESH
            )

    def out_copy(d):
        return remote(
            x_ref, got.at[slot], send.at[d - 1], recv.at[slot], (leaf, row, lax.rem(col + d, cols))
        )

    @pl.when(holds)
    def _():
        pl.semaphore_wait(barrier, cols - 1)
        for d in range(1, cols):
            out_copy(d).start()

    for j in range(per):
        part = slice(j * width, (j + 1) * width)

        @pl.when(row * per + j == col)
        def _():
            o_ref[:, :, part] = x_ref[...]

        @pl.when(row * per + j != col)
        def _():
            remote(
                x_ref, got.at[j], send.at[0], recv.at[j], (leaf, row, row * per + j)
            ).wait_recv()
            o_ref[:, :, part] = got[j]

    @pl.when(holds)
    def _():
        for d in range(1, cols):
            out_copy(d).wait_send()


def leaves_kernel(leaves, x_ref, o_ref, got, send, recv):
    leaf, row, col = place()
    barrier = pltpu.get_barrier_semaphore()
    for d in range(1, leaves):
        pl.semaphore_signal(
            barrier, inc=1, device_id=(lax.rem(leaf + d, leaves), row, col), device_id_type=MESH
        )
    pl.semaphore_wait(barrier, leaves - 1)
    copies = []
    for d in range(1, leaves):
        copies.append(
            remote(
                x_ref, got.at[leaf], send.at[d - 1], recv.at[leaf], (lax.rem(leaf + d, leaves), row, col)
            )
        )
        copies[-1].start()
    o_ref[leaf] = x_ref[...]
    for d in range(1, leaves):
        source = lax.rem(leaf + d, leaves)
        remote(x_ref, got.at[source], send.at[0], recv.at[source], (source, row, col)).wait_recv()
        o_ref[source] = got[source]
    for copy in copies:
        copy.wait_send()


def swap_kernel(x_ref, o_ref, got, send, recv):
    leaf, row, col = place()
    barrier = pltpu.get_barrier_semaphore()
    pl.semaphore_signal(barrier, inc=1, device_id=(leaf, 1 - row, col), device_id_type=MESH)
    pl.semaphore_wait(barrier, 1)
    copy = remote(x_ref, got, send, recv, (leaf, 1 - row, col))
    copy.start()
    copy.wait()
    o_ref[...] = got[...]


def call(kernel, x, out_shape, scratch, collective_id):
    return pl.pallas_call(
        kernel,
        out_shape=jax.ShapeDtypeStruct(out_shape, jnp.float32),
        in_specs=[pl.BlockSpec(memory_space=pltpu.VMEM)],
        out_specs=pl.BlockSpec(memory_space=pltpu.VMEM),
        scratch_shapes=scratch,
        compiler_params=pltpu.CompilerParams(
            collective_id=collective_id, has_side_effects=True, vmem_limit_bytes=40 * 1024 * 1024
        ),
    )(x)


DMA = pltpu.SemaphoreType.DMA


def reduce_chunk(x):
    cols = lax.axis_size("col")
    count, nrhs, rows = x.shape
    shape = (count, nrhs, rows // (cols // 2))
    scratch = [
        pltpu.VMEM((cols,) + shape, jnp.float32),
        pltpu.VMEM(shape, jnp.float32),
        DMA((cols // 2,)),
        DMA((cols,)),
        DMA,
        DMA,
    ]
    return call(functools.partial(reduce_kernel, cols), x, shape, scratch, count)


def gather_rows(x, collective_id):
    cols = lax.axis_size("col")
    per = cols // 2
    count, nrhs, width = x.shape
    scratch = [pltpu.VMEM((per,) + x.shape, jnp.float32), DMA((cols - 1,)), DMA((per,))]
    return call(
        functools.partial(gather_kernel, cols), x, (count, nrhs, width * per), scratch, collective_id
    )


def all_leaves(x):
    leaves = lax.axis_size("leaf")
    shape = (leaves,) + x.shape
    scratch = [pltpu.VMEM(shape, jnp.float32), DMA((leaves - 1,)), DMA((leaves,))]
    return call(functools.partial(leaves_kernel, leaves), x, shape, scratch, 10 + x.shape[0])


def swap(x, collective_id):
    return call(swap_kernel, x, x.shape, [pltpu.VMEM(x.shape, jnp.float32), DMA, DMA], collective_id)


def per_device(
    sec_rhs, sec_inv, sec_low, sec_top, sec_rows, top_rhs, top_inv, top_low, sec_parent, top_parent
):
    parts_row = lax.axis_size("row")
    here_leaf, here_row, here_col = place()
    rows_here = sec_rhs.shape[-1]
    cols_here = sec_inv.shape[-1]
    width = rows_here * parts_row
    blocks = width // BLOCK
    nrhs = sec_rhs.shape[2]
    per = rows_here // cols_here
    first = here_col == 0

    def level(known, partial_value, inverse):
        y = reduce_chunk(jnp.where(first, known, 0.0) - partial_value)
        return reduce_chunk(apply_block(y, inverse))

    right_side = sec_rhs[0]
    inverse = sec_inv[0]
    lower = sec_low[0]
    part = lax.dynamic_slice_in_dim(
        right_side[0:4], lax.rem(here_col, per) * cols_here, cols_here, 2
    )
    theirs = swap(
        lax.dynamic_slice_in_dim(right_side[0:4], lax.rem(here_col, per) * cols_here, cols_here, 2), 20
    )
    y_leaf = jnp.where(here_col // per == here_row, part, theirs)
    x_leaf = reduce_chunk(apply_block(y_leaf, inverse[0:4]))
    acc_mid = apply_block(x_leaf, lower[0:4]).reshape(2, 2, nrhs, rows_here).sum(1)
    acc_root = apply_block(x_leaf, lower[4:8]).sum(0, keepdims=True)
    x_mid = level(right_side[4:6], acc_mid, inverse[4:6])
    acc_root = acc_root + apply_block(x_mid, lower[8:10]).sum(0, keepdims=True)
    x_root = level(right_side[6:7], acc_root, inverse[6:7])
    all_cols = jnp.concatenate([x_leaf, x_mid, x_root], axis=0)
    sec_out = gather_rows(all_cols, 21)[None]

    block_rows = sec_top.shape[2] // BLOCK
    contrib = apply_block(all_cols, sec_top[0]).reshape(7, nrhs, block_rows, BLOCK)
    mine = lax.dynamic_slice_in_dim(sec_rows[0], here_row * block_rows, block_rows, 1)
    one_hot = (mine[:, :, None] == jnp.arange(3 * blocks, dtype=jnp.int32)).astype(jnp.float32)
    one_hot = one_hot.reshape(7, block_rows, 3, parts_row, blocks // parts_row)
    spread = jnp.einsum("jtkl,jknpm->pntml", contrib, one_hot, precision=lax.Precision.HIGH)
    spread = spread.reshape(parts_row, 3, nrhs, rows_here)
    path = lax.dynamic_index_in_dim(spread, here_row, 0, keepdims=False) + swap(
        lax.dynamic_index_in_dim(spread, 1 - here_row, 0, keepdims=False), 22
    )

    section_ids = jnp.arange(sec_parent.shape[0], dtype=jnp.int32)
    nodes = jnp.arange(4, dtype=jnp.int32)
    parent_node = jnp.sum(jnp.where(section_ids == here_leaf, sec_parent, 0))
    grands = jnp.sum(jnp.where(sec_parent[:, None] == nodes[None, :], top_parent[None, :], 0), axis=1)
    grand_node = jnp.sum(jnp.where(section_ids == here_leaf, grands, 0))
    owner = jnp.sum(((grands == grand_node) & (section_ids < here_leaf)).astype(jnp.int32)) == 0

    def pick(array, index, count=1):
        return lax.dynamic_slice_in_dim(array, index, count, 0)

    x_three = level(pick(top_rhs, parent_node), path[0:1], pick(top_inv, parent_node))
    reaches = apply_block(
        jnp.broadcast_to(x_three, (2,) + x_three.shape[1:]), pick(top_low, 2 * parent_node, 2)
    )
    mid_known = jnp.where(first & owner, pick(top_rhs, 4 + grand_node), 0.0)
    y_four = all_leaves(reduce_chunk(mid_known - path[1:2] - reaches[0:1]))
    same = (grands == grand_node)[:, None, None, None]
    y_four = jnp.sum(jnp.where(same, y_four, 0.0), axis=0)
    x_four = reduce_chunk(apply_block(y_four, pick(top_inv, 4 + grand_node)))
    acc_top = apply_block(x_four, pick(top_low, 8 + grand_node))
    root_known = jnp.where(first & (here_leaf == 0), top_rhs[6:7], 0.0)
    y_five = all_leaves(
        reduce_chunk(root_known - path[2:3] - reaches[1:2] - jnp.where(owner, acc_top, 0.0))
    ).sum(0)
    x_five = reduce_chunk(apply_block(y_five, top_inv[6:7]))

    both = all_leaves(jnp.concatenate([x_three, x_four], axis=0))
    tops = []
    for p in range(4):
        tops.append(jnp.sum(jnp.where((sec_parent == p)[:, None, None], both[:, 0], 0.0), axis=0))
    for q in range(2):
        at = (grands == q) & (
            jnp.cumsum((grands == q).astype(jnp.int32)) == 1
        )
        tops.append(jnp.sum(jnp.where(at[:, None, None], both[:, 1], 0.0), axis=0))
    top_out = gather_rows(jnp.concatenate([jnp.stack(tops), x_five], axis=0), 21)
    return (sec_out, top_out)


def solution(mesh):
    placed = (
        P("leaf", None, None, "row"),
        P("leaf", None, "row", "col"),
        P("leaf", None, "row", "col"),
        P("leaf", None, "row", "col"),
        P("leaf", None, None),
        P(None, None, "row"),
        P(None, "row", "col"),
        P(None, "row", "col"),
        P(),
        P(),
    )
    return jax.shard_map(
        per_device,
        mesh=mesh,
        in_specs=placed,
        out_specs=(P("leaf", None, None, "row"), P(None, None, "row")),
        check_vma=False,
    )
```

time: 814 us -> 348 us (0.43); the launches traced: 804 us -> 347 us
  waiting for transfers between devices: 636 us -> 0 us
  Pallas kernels: 0 us -> 268 us
  matrix products: 105 us -> 58.4 us
  other arithmetic: 21.2 us -> 8.31 us
  blocking collectives: 12 us -> 0 us
  between operations: 18.7 us -> 6.89 us
    psum x12 -> x0, waiting for transfers between devices: 578 us -> none  [the longest x6 227 us: solve_level(): x_rows = lax.psum(x_part, 'col')]
    pallas_call x0 -> x18, Pallas kernels: none -> 268 us  [call(): pl.pallas_call(kernel, out_shape=jax.ShapeDtypeStruct(out_shape, jnp.floa...]
    all_gather x6 -> x0, waiting for transfers between devices: 57.8 us -> none  [the longest x3 32.9 us: solve_level(): y_full = lax.all_gather(y_rows, 'row', axis=2, tiled=True)]
    dot_general x12, matrix products: 99.8 us -> 55.8 us  [apply_block(): jnp.einsum('btc,brc->btr', vectors, matrices, precision=lax.Precision.HIGH)]
    all_gather x5 -> x0, blocking collectives: 12 us -> none  [the longest x3 6.68 us: solve_level(): y_full = lax.all_gather(y_rows, 'row', axis=2, tiled=True)]
  transfers between devices with their start and end apart: 18 -> 0, of which waited for: 17 -> 0; matrix products, arithmetic and copies ran while one was open for 2% -> 0% of each run, Pallas kernels for 0% -> 0%
where the time goes in v1:
time: 348 us; the launch traced here: 347 us
  Pallas kernels  268 us (77%)
  matrix products  58.4 us (17%)
  other arithmetic  8.31 us (2%)
  between operations  6.89 us (2%)
  local copies, waits for them, and re-layouts  6.01 us (2%)
    pallas_call x18, Pallas kernels, call(): pl.pallas_call(kernel, out_shape=jax.ShapeDtypeStruct(out_shape, jnp.floa...  268 us
    dot_general x12, matrix products, apply_block(): jnp.einsum('btc,brc->btr', vectors, matrices, precision=lax.Precision.HIGH)  55.8 us

profile of v1, /device:TPU:24, one launch (start us, length us, event | category | flops | bytes accessed | tf_op | source)
XLA Modules:
  0.0 347.3 jit_solution(3215285005963293892)
XLA Ops:
  0.7 0.9 select_reduce_fusion.1
  1.5 0.2 reduce-window.16
  1.7 0.2 reduce-window.17
  1.9 1.3 fusion.92
  8.4 1.3 fusion.96
  10.3 0.7 bitcast_and_fusion.1
  11.1 1.3 slice.78
  12.5 2.0 shard_map.113
  14.5 7.3 %fusion.6.x_ref = f32[4,64,1024]{2,1,0:T(8,128)S(1)} fusion(f32[1,7,1024,512]{3,2,1,0:T(8,128)} %param.11, f32[4,64,512]{2,1,0:T(8,128)S(1)} %dynamic-slice_bitcast_fusion.1.x_ref, f32[4,64,512]{2,1,0:T(8,128)S(1)} %shard_map.113, pred[]{:T(512)S(6)} %eq.141), kind=kOutput, calls=%fused_computation.6 | convolution fusion | flops 805437440 | bytes 10485761 | tf_op jit(solution)/shard_map/btc,brc->btr/dot_general | solution.py:15
  21.8 27.6 %shard_map.114 = f32[4,64,512]{2,1,0:T(8,128)S(1)} custom-call(f32[4,64,1024]{2,1,0:T(8,128)S(1)} %fusion.6.x_ref), custom_call_target="tpu_custom_call" | custom-call | tf_op jit(solution)/shard_map/pallas_call | solution.py:172
  49.4 7.3 %fusion.45 = f32[64,1024]{1,0:T(8,128)S(1)} fusion(f32[4,64,512]{2,1,0:T(8,128)S(1)} %shard_map.114, f32[1,10,1024,512]{3,2,1,0:T(8,128)} %param.12), kind=kOutput, calls=%fused_computation.40 | convolution fusion | flops 805306368 | bytes 9175040 | tf_op jit(solution)/shard_map/btc,brc->btr/dot_general | solution.py:15
  56.8 7.5 %bitcast_reduce_fusion = f32[2,64,1024]{2,1,0:T(8,128)S(1)} fusion(f32[4,64,512]{2,1,0:T(8,128)S(1)} %shard_map.114, f32[1,10,1024,512]{3,2,1,0:T(8,128)} %param.12), kind=kOutput, calls=%fused_computation.49 | convolution fusion | flops 805437440 | bytes 9437184 | tf_op jit(solution)/shard_map/btc,brc->btr/dot_general | solution.py:15
  64.3 1.1 bitcast_subtract_fusion.x_ref
  65.5 16.1 %shard_map.115 = f32[2,64,512]{2,1,0:T(8,128)S(1)} custom-call(f32[2,64,1024]{2,1,0:T(8,128)S(1)} %bitcast_subtract_fusion.x_ref), custom_call_target="tpu_custom_call" | custom-call | tf_op jit(solution)/shard_map/pallas_call | solution.py:172
  81.5 4.4 %fusion.13.x_ref = f32[2,64,1024]{2,1,0:T(8,128)S(1)} fusion(f32[2,64,512]{2,1,0:T(8,128)S(1)} %shard_map.115, f32[1,7,1024,512]{3,2,1,0:T(8,128)} %param.11), kind=kOutput, calls=%fused_computation.13 | convolution fusion | flops 402653184 | bytes 4980736 | tf_op jit(solution)/shard_map/btc,brc->btr/dot_general | solution.py:15
  85.9 15.7 %shard_map.116 = f32[2,64,512]{2,1,0:T(8,128)S(1)} custom-call(f32[2,64,1024]{2,1,0:T(8,128)S(1)} %fusion.13.x_ref), custom_call_target="tpu_custom_call" | custom-call | tf_op jit(solution)/shard_map/pallas_call | solution.py:172
  101.7 4.4 %fusion.69.x_ref = f32[1,64,1024]{2,1,0:T(8,128)S(1)} fusion(f32[64,1024]{1,0:T(8,128)S(1)} %fusion.45, f32[2,64,512]{2,1,0:T(8,128)S(1)} %shard_map.116, f32[1,10,1024,512]{3,2,1,0:T(8,128)} %param.12, f32[1,7,64,1024]{3,2,1,0:T(8,128)} %param.10, pred[]{:T(512)S(6)} %eq.142), kind=kOutput, calls=%fused_computation.48 | convolution fusion | flops 402849792 | bytes 5242881 | tf_op jit(solution)/shard_map/btc,brc->btr/dot_general | solution.py:15
  106.1 10.0 %shard_map.117 = f32[1,64,512]{2,1,0:T(8,128)S(1)} custom-call(f32[1,64,1024]{2,1,0:T(8,128)S(1)} %fusion.69.x_ref), custom_call_target="tpu_custom_call" | custom-call | tf_op jit(solution)/shard_map/pallas_call | solution.py:172
  116.1 2.7 fusion.48.x_ref
  118.8 10.1 %shard_map.118 = f32[1,64,512]{2,1,0:T(8,128)S(1)} custom-call(f32[1,64,1024]{2,1,0:T(8,128)S(1)} %fusion.48.x_ref), custom_call_target="tpu_custom_call" | custom-call | tf_op jit(solution)/shard_map/pallas_call | solution.py:172
  129.0 7.2 %fusion = f32[7,64,1024]{2,1,0:T(8,128)S(1)} fusion(f32[1,7,1024,512]{3,2,1,0:T(8,128)S(1)} %bitcast.197, f32[1,64,512]{2,1,0:T(8,128)S(1)} %shard_map.118, f32[2,64,512]{2,1,0:T(8,128)S(1)} %shard_map.116, f32[4,64,512]{2,1,0:T(8,128)S(1)} %shard_map.114), kind=kOutput, calls=%fused_computation | convolution fusion | flops 1409744896 | bytes 17432576 | tf_op jit(solution)/shard_map/btc,brc->btr/dot_general | solution.py:15
  136.2 0.4 copy.31
  136.6 2.7 fusion.35
  139.3 1.5 reshape.172
  140.9 2.4 shard_map.120
  143.3 0.1 bitcast_add_fusion
  143.4 1.0 slice_subtract_fusion.4.x_ref
  144.4 10.1 %shard_map.121 = f32[1,64,512]{2,1,0:T(8,128)S(1)} custom-call(f32[1,64,1024]{2,1,0:T(8,128)S(1)} %slice_subtract_fusion.4.x_ref), custom_call_target="tpu_custom_call" | custom-call | tf_op jit(solution)/shard_map/pallas_call | solution.py:172
  154.5 2.7 fusion.51.x_ref
  157.1 10.1 %shard_map.122 = f32[1,64,512]{2,1,0:T(8,128)S(1)} custom-call(f32[1,64,1024]{2,1,0:T(8,128)S(1)} %fusion.51.x_ref), custom_call_target="tpu_custom_call" | custom-call | tf_op jit(solution)/shard_map/pallas_call | solution.py:172
  167.2 4.2 %fusion.15 = f32[2,64,1024]{2,1,0:T(8,128)S(1)} fusion(f32[10,1024,512]{2,1,0:T(8,128)} %param.17, s32[]{:T(128)S(6)} %select_n.147, f32[64,512]{1,0:T(8,128)S(1)} %bitcast.195), kind=kOutput, calls=%fused_computation.15 | convolution fusion | flops 402653184 | bytes 4849668 | tf_op jit(solution)/shard_map/btc,brc->btr/dot_general | solution.py:15
  171.4 1.0 slice_subtract_fusion.2.x_ref
  172.5 10.2 %shard_map.123.x_ref = f32[1,64,512]{2,1,0:T(8,128)S(1)} custom-call(f32[1,64,1024]{2,1,0:T(8,128)S(1)} %slice_subtract_fusion.2.x_ref), custom_call_target="tpu_custom_call" | custom-call | tf_op jit(solution)/shard_map/pallas_call | solution.py:172
  182.7 9.5 %shard_map.124 = f32[4,1,64,512]{3,2,1,0:T(8,128)S(1)} custom-call(f32[1,64,512]{2,1,0:T(8,128)S(1)} %shard_map.123.x_ref), custom_call_target="tpu_custom_call" | custom-call | tf_op jit(solution)/shard_map/pallas_call | solution.py:172
  192.2 0.1 select_reduce_fusion
  192.3 2.7 fusion.54.x_ref
  195.0 10.2 %shard_map.125 = f32[1,64,512]{2,1,0:T(8,128)S(1)} custom-call(f32[1,64,1024]{2,1,0:T(8,128)S(1)} %fusion.54.x_ref), custom_call_target="tpu_custom_call" | custom-call | tf_op jit(solution)/shard_map/pallas_call | solution.py:172
  205.2 2.7 fusion.60.x_ref
  207.9 10.7 %shard_map.127.x_ref = f32[1,64,512]{2,1,0:T(8,128)S(1)} custom-call(f32[1,64,1024]{2,1,0:T(8,128)S(1)} %fusion.60.x_ref), custom_call_target="tpu_custom_call" | custom-call | tf_op jit(solution)/shard_map/pallas_call | solution.py:172
  218.7 9.4 %shard_map.128 = f32[4,1,64,512]{3,2,1,0:T(8,128)S(1)} custom-call(f32[1,64,512]{2,1,0:T(8,128)S(1)} %shard_map.127.x_ref), custom_call_target="tpu_custom_call" | custom-call | tf_op jit(solution)/shard_map/pallas_call | solution.py:172
  228.1 2.7 fusion.57.x_ref
  230.8 10.1 %shard_map.129 = f32[1,64,512]{2,1,0:T(8,128)S(1)} custom-call(f32[1,64,1024]{2,1,0:T(8,128)S(1)} %fusion.57.x_ref), custom_call_target="tpu_custom_call" | custom-call | tf_op jit(solution)/shard_map/pallas_call | solution.py:172
  240.9 15.1 %shard_map.126 = f32[4,2,64,512]{3,2,1,0:T(8,128)S(1)} custom-call(f32[2,64,512]{2,1,0:T(8,128)S(1)} %pad_maximum_fusion.1.x_ref), custom_call_target="tpu_custom_call" | custom-call | tf_op jit(solution)/shard_map/pallas_call | solution.py:172
  256.1 0.3 fusion.77
  256.5 44.3 %shard_map.130 = f32[7,64,1024]{2,1,0:T(8,128)S(1)} custom-call(f32[7,64,512]{2,1,0:T(8,128)S(1)} %constant_dynamic-update-slice_fusion.x_ref), custom_call_target="tpu_custom_call" | custom-call | tf_op jit(solution)/shard_map/pallas_call | solution.py:172
  300.9 43.9 %shard_map.119 = f32[7,64,1024]{2,1,0:T(8,128)S(1)} custom-call(f32[7,64,512]{2,1,0:T(8,128)S(1)} %pad_maximum_fusion.x_ref), custom_call_target="tpu_custom_call" | custom-call | tf_op jit(solution)/shard_map/pallas_call | solution.py:172
  344.8 1.2 copy.42
  346.1 1.2 copy.43
  (29 shorter events, 0.4 us)
Async XLA Ops:
  0.6 10.4 %copy-start = (s32[1,7,16]{2,0,1:T(1,128)S(1)}, s32[1,7,16]{2,0,1:T(1,128)}, u32[]{:S(2)}) copy-start(s32[1,7,16]{2,0,1:T(1,128)} %param.14) | copy-start | bytes 1348
  56.8 72.2 %slice-start = ((s8[14680064]{0:T(1024)(128)(4,1)}), s8[4194304]{0:T(1024)(128)(4,1)S(1)}, s32[]{:S(2)}) async-start(s8[14680064]{0:T(1024)(128)(4,1)} %bitcast.196), calls=%async_computation | async-start | bytes 8388608
  56.8 72.2 %slice-start.1 = ((s8[14680064]{0:T(1024)(128)(4,1)}), s8[4194304]{0:T(1024)(128)(4,1)S(1)}, s32[]{:S(2)}) async-start(s8[14680064]{0:T(1024)(128)(4,1)} %bitcast.196), calls=%async_computation.1 | async-start | bytes 8388608
  81.5 47.5 %slice-start.2 = ((s8[14680064]{0:T(1024)(128)(4,1)}), s8[4194304]{0:T(1024)(128)(4,1)S(1)}, s32[]{:S(2)}) async-start(s8[14680064]{0:T(1024)(128)(4,1)} %bitcast.196), calls=%async_computation.2 | async-start | bytes 8388608
  101.7 27.3 %slice-start.3 = ((s8[14680064]{0:T(1024)(128)(4,1)}), s8[2097152]{0:T(1024)(128)(4,1)S(1)}, s32[]{:S(2)}) async-start(s8[14680064]{0:T(1024)(128)(4,1)} %bitcast.196), calls=%async_computation.3 | async-start | bytes 4194304
  300.9 46.4 %copy-start.1 = (s32[1,7,16]{2,0,1:T(1,128)S(1)}, s32[1,7,16]{2,0,1:T(1,128)}, u32[]{:S(2)}) copy-start(s32[1,7,16]{2,0,1:T(1,128)} %param.14) | copy-start | bytes 1348
